TPU v7x, 256 devices: a whole 4x4x8 slice. The times are simulated.
256 devices in a mesh: dp: 8 (over y, core), seq: 32 (over x, z).
Axes of the slice: x: 4, y: 4, z: 8, core: 2. Of those that a mesh axis runs over, the one named last changes fastest.
Arguments:
- queries: bfloat16 [32768, 4096], P(('dp', 'seq')), may hold values from -8 to 8
- keys: bfloat16 [32768, 512], P(('dp', 'seq')), may hold values from -8 to 8
- values: bfloat16 [32768, 512], P(('dp', 'seq')), may hold values from -6 to 6
- out_grad: bfloat16 [32768, 4096], P(('dp', 'seq')), may hold values from -6 to 6
- doc_lengths: int32 [64], replicated, may hold values from 1 to 1024, as said below
Outputs:
- attn_out: bfloat16 [32768, 4096], P(('dp', 'seq'))
- query_grad: bfloat16 [32768, 4096], P(('dp', 'seq'))
- gradient_keys: bfloat16 [32768, 512], P(('dp', 'seq'))
- gradient_values: bfloat16 [32768, 512], P(('dp', 'seq'))
Inputs may be any that keep to these rules, and one draw needn't show every extreme that they name: `doc_lengths`: the 64 lengths sum to 32768. The documents come in 8 groups of 8, one group for each block of 4096 rows; the first of each group is 1024 rows long and starts at row 0 in the first block, exactly 512 rows before the second block, and 256 to 512 rows before every later block.
All inputs are finite; a program needn't handle non-finite values.
Results may differ from a plain program's by a relative error of at most 0.0085.
Values may be sent and summed in bfloat16 or wider, within the bound.
A program may use at most 64 MiB of HBM per device.

v0:
```python
import math

import jax
import jax.numpy as jnp
from jax import lax
from jax.sharding import PartitionSpec as P

QUERY_HEADS = 32
KEY_VALUE_HEADS = 4
HEAD_WIDTH = 128


masked_score = -1e30


def from_behind(block, axis, distance):
    devices = range(lax.axis_size(axis))
    route = [(i - distance, i) for i in devices if i - distance in devices]
    return lax.ppermute(block, axis, route)


def doc_index(positions, starts):
    hits = (starts[None, :] <= positions[:, None]).astype(jnp.int32)
    return jnp.sum(hits, axis=1) - 1


def attend_block(
    query_block,
    grad_block,
    query_pos,
    query_doc,
    key_window,
    value_window,
    key_pos,
    key_doc,
    score_scale,
):
    scores = jnp.dot(query_block, key_window.T, preferred_element_type=jnp.float32) * score_scale
    allowed = (key_doc[None, :] == query_doc[:, None]) & (key_pos[None, :] <= query_pos[:, None])
    scores = jnp.where(allowed, scores, masked_score)
    highest = jnp.max(scores, axis=1, keepdims=True)
    weights = jnp.where(allowed, jnp.exp(scores - highest), 0.0)
    probs = weights / jnp.sum(weights, axis=1, keepdims=True)
    probs_low = probs.astype(jnp.bfloat16)
    attended = jnp.dot(probs_low, value_window, preferred_element_type=jnp.float32).astype(
        jnp.bfloat16
    )
    stored = lax.optimization_barrier(attended).astype(jnp.float32)
    delta = jnp.sum(grad_block.astype(jnp.float32) * stored, axis=1, keepdims=True)
    dprobs = jnp.dot(grad_block, value_window.T, preferred_element_type=jnp.float32)
    dscores_low = (probs * (dprobs - delta)).astype(jnp.bfloat16)
    query_part = (
        jnp.dot(dscores_low, key_window, preferred_element_type=jnp.float32) * score_scale
    ).astype(jnp.bfloat16)
    key_part = jnp.dot(dscores_low.T, query_block, preferred_element_type=jnp.float32) * score_scale
    value_part = jnp.dot(probs_low.T, grad_block, preferred_element_type=jnp.float32)
    return (attended, query_part, key_part, value_part)


def sweep(
    query_rows, grad_rows, key_rows, value_rows, key_pos, key_doc, qblock, window, score_scale
):
    query_count = query_rows.shape[0]
    key_count = key_rows.shape[0]
    offset = key_count - query_count
    depth = query_rows.shape[1]
    query_pos = key_pos[offset:]
    query_doc = key_doc[offset:]

    def advance(number, totals):
        attended_all, qgrad_all, kgrad_all, vgrad_all = totals
        row_start = (number * qblock).astype(jnp.int32)
        window_start = jnp.maximum(row_start + offset + qblock - window, 0)
        query_block = lax.dynamic_slice_in_dim(query_rows, row_start, qblock, 0)
        grad_block = lax.dynamic_slice_in_dim(grad_rows, row_start, qblock, 0)
        block_pos = lax.dynamic_slice_in_dim(query_pos, row_start, qblock, 0)
        block_doc = lax.dynamic_slice_in_dim(query_doc, row_start, qblock, 0)
        key_window = lax.dynamic_slice_in_dim(key_rows, window_start, window, 0)
        value_window = lax.dynamic_slice_in_dim(value_rows, window_start, window, 0)
        window_pos = lax.dynamic_slice_in_dim(key_pos, window_start, window, 0)
        window_doc = lax.dynamic_slice_in_dim(key_doc, window_start, window, 0)
        attended, query_part, key_part, value_part = attend_block(
            query_block,
            grad_block,
            block_pos,
            block_doc,
            key_window,
            value_window,
            window_pos,
            window_doc,
            score_scale,
        )
        attended_all = lax.dynamic_update_slice_in_dim(attended_all, attended, row_start, 0)
        qgrad_all = lax.dynamic_update_slice_in_dim(qgrad_all, query_part, row_start, 0)
        kgrad_all = lax.dynamic_update_slice_in_dim(
            kgrad_all,
            lax.dynamic_slice_in_dim(kgrad_all, window_start, window, 0) + key_part,
            window_start,
            0,
        )
        vgrad_all = lax.dynamic_update_slice_in_dim(
            vgrad_all,
            lax.dynamic_slice_in_dim(vgrad_all, window_start, window, 0) + value_part,
            window_start,
            0,
        )
        return (attended_all, qgrad_all, kgrad_all, vgrad_all)

    initial = (
        jnp.zeros((query_count, depth), jnp.bfloat16),
        jnp.zeros((query_count, depth), jnp.bfloat16),
        jnp.zeros((key_count, depth), jnp.float32),
        jnp.zeros((key_count, depth), jnp.float32),
    )
    return lax.fori_loop(0, query_count // qblock, advance, initial)


def per_device(queries, keys, values, out_grad, doc_lengths):
    seq_count = lax.axis_size("seq")
    token_rows = queries.shape[0]
    group = token_rows * seq_count
    heads_local = QUERY_HEADS // seq_count
    group_share = QUERY_HEADS // KEY_VALUE_HEADS
    longest = group // 4
    reach = longest // 2
    qblock = min(512, group)
    window = min(qblock + longest, reach + group)
    score_scale = 1.0 / math.sqrt(HEAD_WIDTH)
    head_queries, head_grads = (
        lax.all_to_all(queries, "seq", split_axis=1, concat_axis=0, tiled=True),
        lax.all_to_all(out_grad, "seq", split_axis=1, concat_axis=0, tiled=True),
    )
    group_keys, group_values = (
        lax.all_gather(keys, "seq", axis=0, tiled=True),
        lax.all_gather(values, "seq", axis=0, tiled=True),
    )
    first_head = lax.axis_index("seq") * heads_local
    column = (first_head + 0) // group_share * HEAD_WIDTH
    key_parts = lax.dynamic_slice_in_dim(group_keys, column, HEAD_WIDTH, 1)
    value_parts = lax.dynamic_slice_in_dim(group_values, column, HEAD_WIDTH, 1)
    before_keys, before_values = from_behind(
        (key_parts[group - reach :], value_parts[group - reach :]), "dp", 1
    )
    full_keys = jnp.concatenate([before_keys, key_parts], axis=0)
    full_values = jnp.concatenate([before_values, value_parts], axis=0)
    starts = jnp.cumsum(doc_lengths) - doc_lengths
    anchor = lax.axis_index("dp") * group - reach
    key_pos = anchor + jnp.arange(reach + group, dtype=jnp.int32)
    key_doc = doc_index(key_pos, starts)
    attended, qgrads, key_gradients, value_gradients = sweep(
        head_queries,
        head_grads,
        full_keys,
        full_values,
        key_pos,
        key_doc,
        qblock,
        window,
        score_scale,
    )
    later_keys, later_values = from_behind(
        (key_gradients[:reach], value_gradients[:reach]), "dp", -1
    )
    own_keys = key_gradients[reach:]
    own_values = value_gradients[reach:]
    own_keys = jnp.concatenate(
        [own_keys[: group - reach], own_keys[group - reach :] + later_keys], axis=0
    )
    own_values = jnp.concatenate(
        [own_values[: group - reach], own_values[group - reach :] + later_values], axis=0
    )
    attn_out, query_grad = (
        lax.all_to_all(attended, "seq", split_axis=0, concat_axis=1, tiled=True),
        lax.all_to_all(qgrads, "seq", split_axis=0, concat_axis=1, tiled=True),
    )
    key_summands, value_summands = (
        lax.all_to_all(own_keys, "seq", split_axis=0, concat_axis=1, tiled=True),
        lax.all_to_all(own_values, "seq", split_axis=0, concat_axis=1, tiled=True),
    )
    gradient_keys = (
        jnp.sum(key_summands.reshape(token_rows, KEY_VALUE_HEADS, group_share, HEAD_WIDTH), axis=2)
        .reshape(token_rows, KEY_VALUE_HEADS * HEAD_WIDTH)
        .astype(jnp.bfloat16)
    )
    gradient_values = (
        jnp.sum(
            value_summands.reshape(token_rows, KEY_VALUE_HEADS, group_share, HEAD_WIDTH), axis=2
        )
        .reshape(token_rows, KEY_VALUE_HEADS * HEAD_WIDTH)
        .astype(jnp.bfloat16)
    )
    return (attn_out, query_grad, gradient_keys, gradient_values)


def solution(mesh):
    return jax.shard_map(
        per_device,
        mesh=mesh,
        in_specs=(
            P(("dp", "seq"), None),
            P(("dp", "seq"), None),
            P(("dp", "seq"), None),
            P(("dp", "seq"), None),
            P(),
        ),
        out_specs=(
            P(("dp", "seq"), None),
            P(("dp", "seq"), None),
            P(("dp", "seq"), None),
            P(("dp", "seq"), None),
        ),
        check_vma=False,
    )
```

profile of v0, /device:TPU:8, one launch (start us, length us, event | category | flops | bytes accessed | tf_op | source)
XLA Modules:
  0.0 589.9 jit_solution(7916396292304105545)
XLA Ops:
  10.0 11.4 %all-to-all-start = ((bf16[128,32,128]{2,0,1:T(8,128)(2,1)}), bf16[128,32,128]{2,0,1:T(8,128)(2,1)}, u32[]{:S(2)}, u32[]{:S(2)}) async-start(bf16[128,32,128]{2,0,1:T(8,128)(2,1)} %copy_bitcast_fusion.1), calls=%async_computation | async-start | bytes 2097152 | tf_op jit(solution)/shard_map/all_to_all | solution.py:130
  23.3 76.5 %all-gather.3.cloned.1.call-done = bf16[4096,512]{1,0:T(8,128)(2,1)} async-done(((bf16[128,512]{1,0:T(8,128)(2,1)}), bf16[4096,512]{1,0:T(8,128)(2,1)}) %all-gather.3.cloned.1.call-update) | async-done | bytes 4194320 | tf_op jit(solution)/shard_map/all_gather | solution.py:134
  102.6 78.8 %all-gather.5.cloned.1.call-done = bf16[4096,512]{1,0:T(8,128)(2,1)} async-done(((bf16[128,512]{1,0:T(8,128)(2,1)}), bf16[4096,512]{1,0:T(8,128)(2,1)}) %all-gather.5.cloned.1.call-update) | async-done | bytes 4194320 | tf_op jit(solution)/shard_map/all_gather | solution.py:135
  184.3 6.0 %all-to-all-start.1 = ((bf16[128,32,128]{2,0,1:T(8,128)(2,1)}), bf16[128,32,128]{2,0,1:T(8,128)(2,1)}, u32[]{:S(2)}, u32[]{:S(2)}) async-start(bf16[128,32,128]{2,0,1:T(8,128)(2,1)} %copy_bitcast_fusion), calls=%async_computation.1 | async-start | bytes 2097152 | tf_op jit(solution)/shard_map/all_to_all | solution.py:131
  195.2 23.7 %all-to-all-done.1 = bf16[128,32,128]{2,0,1:T(8,128)(2,1)} async-done(((bf16[128,32,128]{2,0,1:T(8,128)(2,1)}), bf16[128,32,128]{2,0,1:T(8,128)(2,1)}, u32[]{:S(2)}, u32[]{:S(2)}) %all-to-all-start.1) | async-done | bytes 1048608 | tf_op jit(solution)/shard_map/all_to_all | solution.py:131
  224.2 178.4 %while.23 = (s32[]{:T(128)}, bf16[4096,128]{1,0:T(8,128)(2,1)}, bf16[4096,128]{1,0:T(8,128)(2,1)}, f32[4608,128]{1,0:T(8,128)}, f32[4608,128]{1,0:T(8,128)}, /*i...) while((s32[]{:T(128)}, bf16[4096,128]{1,0:T(8,128)(2,1)}, ...), condition=%wide.region_6.7_spmd, body=%wide.region_2.6_spmd.sunk | while | flops 1227094528 | bytes 35879220 | solution.py:115
  243.2 3.5 dynamic_update_slice.61
  306.9 3.5 dynamic_update_slice.60
  310.4 3.5 dynamic_update_slice.61
  329.4 3.5 dynamic_update_slice.60
  332.9 3.5 dynamic_update_slice.61
  351.8 3.5 dynamic_update_slice.60
  355.3 3.5 dynamic_update_slice.61
  374.2 3.5 dynamic_update_slice.60
  377.7 3.5 dynamic_update_slice.61
  402.6 35.6 %all_to_all.108 = bf16[32,128,128]{2,1,0:T(8,128)(2,1)} all-to-all(bf16[32,128,128]{2,1,0:T(8,128)(2,1)} %bitcast.8), channel_id=1, replica_groups=mesh['dp'=8,'seq'=32] {'seq'}, dimensions={0} | all-to-all | bytes 2097152 | tf_op jit(solution)/shard_map/all_to_all | solution.py:174
  438.2 5.2 all-to-all-start.2
  445.6 3.7 collective-permute-done.2
  450.9 20.9 %all-to-all-done.2 = bf16[32,128,128]{2,1,0:T(8,128)(2,1)} async-done(((bf16[32,128,128]{2,1,0:T(8,128)(2,1)}), bf16[32,128,128]{2,1,0:T(8,128)(2,1)}, u32[]{:S(2)}, u32[]{:S(2)}) %all-to-all-start.2) | async-done | bytes 1048608 | tf_op jit(solution)/shard_map/all_to_all | solution.py:173
  471.7 5.0 all-to-all-start.4
  478.9 3.7 collective-permute-done.3
  484.1 42.3 %all-to-all-done.4 = f32[32,128,128]{2,1,0:T(8,128)} async-done(((f32[32,128,128]{2,1,0:T(8,128)}), f32[32,128,128]{2,1,0:T(8,128)}, u32[]{:S(2)}, u32[]{:S(2)}) %all-to-all-start.4) | async-done | bytes 2097184 | tf_op jit(solution)/shard_map/all_to_all | solution.py:177
  526.4 6.0 %all-to-all-start.5 = ((f32[32,128,128]{2,1,0:T(8,128)}), f32[32,128,128]{2,1,0:T(8,128)S(1)}, u32[]{:S(2)}, u32[]{:S(2)}) async-start(f32[32,128,128]{2,1,0:T(8,128)} %bitcast.15), calls=%async_computation.5 | async-start | bytes 4194304 | tf_op jit(solution)/shard_map/all_to_all | solution.py:178
  544.1 38.0 %all-to-all-done.5 = f32[32,128,128]{2,1,0:T(8,128)S(1)} async-done(((f32[32,128,128]{2,1,0:T(8,128)}), f32[32,128,128]{2,1,0:T(8,128)S(1)}, u32[]{:S(2)}, u32[]{:S(2)}) %all-to-all-start.5) | async-done | bytes 2097184 | tf_op jit(solution)/shard_map/all_to_all | solution.py:178
  (171 shorter events, 187.0 us)
Async XLA Ops:
  7.2 1.5 copy-start
  7.2 14.3 %copy-start.4 = (s32[64]{0:T(128)S(1)}, s32[64]{0:T(128)}, u32[]{:S(2)}) copy-start(s32[64]{0:T(128)} %param.11) | copy-start | bytes 772
  7.2 92.6 %all-gather.3.cloned.1.call-start = ((), (), s32[]{:S(2)}) async-start(), calls=%async_computation.6 | async-start | bytes 4325376 | tf_op jit(solution)/shard_map/all_gather | solution.py:134
  7.9 14.1 %copy-start.3 = (bf16[128,4096]{1,0:T(8,128)(2,1)S(1)}, bf16[128,4096]{1,0:T(8,128)(2,1)}, u32[]{:S(2)}) copy-start(bf16[128,4096]{1,0:T(8,128)(2,1)} %param.10) | copy-start | bytes 3145732
  7.9 173.5 %all-gather.5.cloned.1.call-start = ((), (), s32[]{:S(2)}) async-start(), calls=%async_computation.7 | async-start | bytes 4325376 | tf_op jit(solution)/shard_map/all_gather | solution.py:135
  10.0 174.3 %all-to-all-start = ((bf16[128,32,128]{2,0,1:T(8,128)(2,1)}), bf16[128,32,128]{2,0,1:T(8,128)(2,1)}, u32[]{:S(2)}, u32[]{:S(2)}) async-start(bf16[128,32,128]{2,0,1:T(8,128)(2,1)} %copy_bitcast_fusion.1), calls=%async_computation | async-start | bytes 2097152 | tf_op jit(solution)/shard_map/all_to_all | solution.py:130
  100.7 92.2 %collective-permute-start = (bf16[512,128]{1,0:T(8,128)(2,1)S(1)}, bf16[512,128]{1,0:T(8,128)(2,1)S(1)}, u32[]{:S(2)}, u32[]{:S(2)}) collective-permute-start(bf16[512,128]{1,0:T(8,128)(2,1)S(1)} %dynamic-slice), channel_id=1, source_target_pairs={{0,32},{32,64},{64,96},{96,128},{128,160},{160,192},{192,224},{1,3... | collective-permute-start | bytes 393224 | tf_op jit(solution)/shard_map/ppermute | solution.py:19
  182.3 11.7 %collective-permute-start.1 = (bf16[512,128]{1,0:T(8,128)(2,1)S(1)}, bf16[512,128]{1,0:T(8,128)(2,1)S(1)}, u32[]{:S(2)}, u32[]{:S(2)}) collective-permute-start(bf16[512,128]{1,0:T(8,128)(2,1)S(1)} %dynamic-slice.1), channel_id=1, source_target_pairs={{0,32},{32,64},{64,96},{96,128},{128,160},{160,192},{192,224},{1,3... | collective-permute-start | bytes 393224 | tf_op jit(solution)/shard_map/ppermute | solution.py:19
  184.3 34.6 %all-to-all-start.1 = ((bf16[128,32,128]{2,0,1:T(8,128)(2,1)}), bf16[128,32,128]{2,0,1:T(8,128)(2,1)}, u32[]{:S(2)}, u32[]{:S(2)}) async-start(bf16[128,32,128]{2,0,1:T(8,128)(2,1)} %copy_bitcast_fusion), calls=%async_computation.1 | async-start | bytes 2097152 | tf_op jit(solution)/shard_map/all_to_all | solution.py:131
  402.6 40.8 %copy-start.1 = (f32[4608,128]{1,0:T(8,128)S(1)}, f32[4608,128]{1,0:T(8,128)}, u32[]{:S(2)}) copy-start(f32[4608,128]{1,0:T(8,128)} %get-tuple-element.412) | copy-start | bytes 7077892
  438.2 33.5 %all-to-all-start.2 = ((bf16[32,128,128]{2,1,0:T(8,128)(2,1)}), bf16[32,128,128]{2,1,0:T(8,128)(2,1)}, u32[]{:S(2)}, u32[]{:S(2)}) async-start(bf16[32,128,128]{2,1,0:T(8,128)(2,1)} %bitcast.5), calls=%async_computation.2 | async-start | bytes 2097152 | tf_op jit(solution)/shard_map/all_to_all | solution.py:173
  443.5 5.8 collective-permute-start.2
  450.9 25.9 %copy-start.2 = (f32[4608,128]{1,0:T(8,128)S(1)}, f32[4608,128]{1,0:T(8,128)}, u32[]{:S(2)}) copy-start(f32[4608,128]{1,0:T(8,128)} %get-tuple-element.413) | copy-start | bytes 7077892
  471.7 54.7 %all-to-all-start.4 = ((f32[32,128,128]{2,1,0:T(8,128)}), f32[32,128,128]{2,1,0:T(8,128)}, u32[]{:S(2)}, u32[]{:S(2)}) async-start(f32[32,128,128]{2,1,0:T(8,128)} %bitcast.43), calls=%async_computation.4 | async-start | bytes 4194304 | tf_op jit(solution)/shard_map/all_to_all | solution.py:177
  476.8 5.8 collective-permute-start.3
  526.4 55.7 %all-to-all-start.5 = ((f32[32,128,128]{2,1,0:T(8,128)}), f32[32,128,128]{2,1,0:T(8,128)S(1)}, u32[]{:S(2)}, u32[]{:S(2)}) async-start(f32[32,128,128]{2,1,0:T(8,128)} %bitcast.15), calls=%async_computation.5 | async-start | bytes 4194304 | tf_op jit(solution)/shard_map/all_to_all | solution.py:178
Sparse Core Ops, SparseCore 0:
  10.6 89.1 all-gather.2
  102.4 78.9 all-gather.4
where the time goes:
time: 593 us; the launch traced here: 590 us
  waiting for transfers between devices  289 us (49%)
  matrix products  95.7 us (16%)
  local copies, waits for them, and re-layouts  80.7 us (14%)
  starting transfers between devices  41.5 us (7%)
  blocking collectives  35.6 us (6%)
  other arithmetic  32.8 us (6%)
  between operations  14.3 us (2%)
    all_gather x1, waiting for transfers between devices, per_device(): lax.all_gather(values, 'seq', axis=0, tiled=True)  78.8 us
    all_gather x1, waiting for transfers between devices, per_device(): lax.all_gather(keys, 'seq', axis=0, tiled=True)  76.5 us
    all_to_all x1, waiting for transfers between devices, per_device(): lax.all_to_all(own_keys, 'seq', split_axis=0, concat_axis=1, tiled=True)  42.3 us
    all_to_all x1, waiting for transfers between devices, per_device(): lax.all_to_all(own_values, 'seq', split_axis=0, concat_axis=1, tiled=True)  38 us
    all_to_all x1, blocking collectives, per_device(): lax.all_to_all(qgrads, 'seq', split_axis=0, concat_axis=1, tiled=True)  35.6 us
    dynamic_update_slice x8, local copies, waits for them, and re-layouts, advance(): lax.dynamic_update_slice_in_dim(vgrad_all, lax.dynamic_slice_in_dim(vgrad...  27.4 us
    dynamic_update_slice x8, local copies, waits for them, and re-layouts, advance(): lax.dynamic_update_slice_in_dim(kgrad_all, lax.dynamic_slice_in_dim(kgrad...  27.4 us
    all_to_all x1, waiting for transfers between devices, per_device(): lax.all_to_all(out_grad, 'seq', split_axis=1, concat_axis=0, tiled=True)  23.7 us
  transfers between devices with their start and end apart: 11, of which 8 were waited for; matrix products, arithmetic and copies ran while one was open for 4% of the time, Pallas kernels for 0%

commit v1 on v0

v1 whole, which is shorter than its diff:
```python
import functools
import math

import jax
import jax.numpy as jnp
from jax import lax
from jax.experimental import pallas as pl
from jax.experimental.pallas import tpu as pltpu
from jax.sharding import PartitionSpec as P

MESH = pl.DeviceIdType.MESH
WIDTH = 128
REACH = 8
FORWARD = 4
MASKED = -1e30
BF16 = jnp.bfloat16
F32 = jnp.float32


def nt(a, b):
    return lax.dot_general(a, b, (((1,), (1,)), ((), ())), preferred_element_type=F32)


def nn(a, b):
    return lax.dot_general(a, b, (((1,), (0,)), ((), ())), preferred_element_type=F32)


def kernel(
    dims,
    lengths,
    queries,
    keys,
    values,
    out_grad,
    attended,
    query_grad,
    key_grad,
    value_grad,
    q_s,
    do_s,
    kv_s,
    o_s,
    dq_s,
    bias_s,
    t_s,
    dp_s,
    p_s,
    ds_s,
    part_s,
    own_s,
    back_s,
    fin_s,
    load_sem,
    store_sem,
    in_send,
    in_recv,
    out_send,
    out_recv,
):
    n_dp, n_seq, rows, heads, kv_heads = dims
    share = heads // kv_heads
    blocks = REACH + 1
    span = blocks * rows
    total = n_dp * n_seq
    scale = 1.0 / math.sqrt(WIDTH)
    me = lax.axis_index("dp") * n_seq + lax.axis_index("seq")

    def device(distance):
        flat = lax.rem(me + (distance + total), total)
        return (flat // n_seq, lax.rem(flat, n_seq))

    after, before, far_after, far_before = device(1), device(-1), device(REACH), device(-REACH)

    def own_kv(g):
        cols = pl.ds(g * WIDTH, WIDTH)
        return (
            pltpu.make_async_copy(keys.at[:, cols], kv_s.at[g, REACH, 0], load_sem.at[2 * heads + 2 * g]),
            pltpu.make_async_copy(
                values.at[:, cols], kv_s.at[g, REACH, 1], load_sem.at[2 * heads + 2 * g + 1]
            ),
        )

    def own_q(h):
        cols = pl.ds(pl.multiple_of(h * WIDTH, WIDTH), WIDTH)
        to = pl.ds(pl.multiple_of(h * rows, rows), rows)
        return (
            pltpu.make_async_copy(queries.at[:, cols], q_s.at[to], load_sem.at[2 * h]),
            pltpu.make_async_copy(out_grad.at[:, cols], do_s.at[to], load_sem.at[2 * h + 1]),
        )

    for g in range(kv_heads):
        for copy in own_kv(g):
            copy.start()

    @pl.loop(0, heads)
    def _(h):
        for copy in own_q(h):
            copy.start()

    barrier = pltpu.get_barrier_semaphore()
    for peer in (after, before, far_after, far_before):
        pl.semaphore_signal(barrier, inc=1, device_id=peer, device_id_type=MESH)
    pl.semaphore_wait(barrier, 4)

    def hand(g, k, to, peer, send):
        return pltpu.make_async_remote_copy(
            src_ref=kv_s.at[g, REACH - k],
            dst_ref=kv_s.at[g, REACH - to],
            send_sem=in_send.at[g, send],
            recv_sem=in_recv.at[g, to],
            device_id=peer,
            device_id_type=MESH,
        )

    def give_first(g):
        return hand(g, 0, REACH, far_after, REACH + 1)

    def give_up(g, k):
        return hand(g, k, k + 1, after, k)

    def give_down(g, k):
        return hand(g, k, k - 1, before, k)

    for g in range(kv_heads):
        for copy in own_kv(g):
            copy.wait()
        give_up(g, 0).start()
        give_first(g).start()

    row_pos = me * rows + lax.broadcasted_iota(jnp.int32, (1, rows), 1)

    def find(d, carry):
        start, cum = carry
        return jnp.where(row_pos >= cum, cum, start), cum + lengths[d]

    doc_start, _ = lax.fori_loop(
        0, lengths.shape[0], find, (jnp.zeros((1, rows), jnp.int32), jnp.int32(0))
    )
    for b in range(blocks):
        key_pos = (me + (b - REACH)) * rows + lax.broadcasted_iota(jnp.int32, (rows, rows), 0)
        allowed = (key_pos >= doc_start) & (key_pos <= row_pos)
        bias_s[b * rows : (b + 1) * rows, :] = jnp.where(allowed, 0.0, MASKED)

    order = sorted(
        ((s, g) for s in range(1, FORWARD) for g in range(kv_heads)), key=lambda sg: sg[0] * 2.3 + sg[1]
    )
    for s, g in order:
        give_first(g).wait_recv() if s == 1 else give_down(g, REACH + 2 - s).wait_recv()
        give_down(g, REACH + 1 - s).start()
        give_up(g, s - 1).wait_recv()
        give_up(g, s).start()

    @pl.loop(0, heads)
    def _(h):
        for copy in own_q(h):
            copy.wait()

    def back(g, way, k, to, peer):
        return pltpu.make_async_remote_copy(
            src_ref=part_s.at[g, k],
            dst_ref=back_s.at[g, way, to],
            send_sem=out_send.at[g, k],
            recv_sem=out_recv.at[g, way, to],
            device_id=peer,
            device_id_type=MESH,
        )

    def back_down(g, k):
        return back(g, 0, k, k - 1, before)

    def back_up(g, k):
        return back(g, 1, k, k + 1, after) if k < REACH else back(g, 1, k, 0, far_before)

    def stage(g, s):
        low, high = FORWARD - s, FORWARD + 1 + s
        if s:
            back_down(g, low + 1).wait_recv()
            part_s[g, low] = (part_s[g, low].astype(F32) + back_s[g, 0, low].astype(F32)).astype(BF16)
        back_down(g, low).start()
        if s:
            back_up(g, high - 1).wait_recv()
            part_s[g, high] = (part_s[g, high].astype(F32) + back_s[g, 1, high].astype(F32)).astype(BF16)
        back_up(g, high).start()

    def last_stage(g):
        back_down(g, 1).wait_recv()
        back_up(g, REACH).wait_recv()
        total_kv = own_s[g] + back_s[g, 0, 0].astype(F32) + back_s[g, 1, 0].astype(F32)
        cols = pl.ds(pl.multiple_of(g * WIDTH, WIDTH), WIDTH)
        fin_s[0, :, cols] = total_kv[0].astype(BF16)
        fin_s[1, :, cols] = total_kv[1].astype(BF16)

    factor = scale * math.log2(math.e)

    def compute(g):
        k_all = kv_s[g, :, 0].reshape(span, WIDTH)
        v_all = kv_s[g, :, 1].reshape(span, WIDTH)
        for pair in range(share // 2):
            slot = pair % 2
            at = pl.ds(pl.multiple_of(g * (share * rows) + pair * 2 * rows, 2 * rows), 2 * rows)
            q_pair, do_pair = q_s[at], do_s[at]
            cols = slice(pair * 2 * rows, (pair + 1) * 2 * rows)
            high = jnp.full((8, 2 * rows), MASKED, F32)
            for b in range(blocks):
                r = slice(b * rows, (b + 1) * rows)
                bias = bias_s[r, :]
                t = nt(kv_s[g, b, 0], q_pair) * factor + jnp.concatenate([bias, bias], axis=1)
                t_s[slot, r, :] = t
                high = jnp.maximum(high, jnp.max(t.reshape(rows // 8, 8, 2 * rows), axis=0))
            high = jnp.max(high, axis=0, keepdims=True)
            norm = jnp.zeros((8, 2 * rows), F32)
            mix = jnp.zeros((8, 2 * rows), F32)
            for b in range(blocks):
                r = slice(b * rows, (b + 1) * rows)
                w = jnp.exp2(t_s[slot, r, :] - high)
                dp = nt(kv_s[g, b, 1], do_pair)
                t_s[slot, r, :] = w
                dp_s[slot, r, :] = dp
                norm += jnp.sum(w.reshape(rows // 8, 8, 2 * rows), axis=0)
                mix += jnp.sum((w * dp).reshape(rows // 8, 8, 2 * rows), axis=0)
            inverse = 1.0 / jnp.sum(norm, axis=0, keepdims=True)
            delta = jnp.sum(mix, axis=0, keepdims=True) * inverse
            for b in range(blocks):
                r = slice(b * rows, (b + 1) * rows)
                p = t_s[slot, r, :] * inverse
                p_s[r, cols] = p.astype(BF16)
                ds_s[r, cols] = (p * (dp_s[slot, r, :] - delta)).astype(BF16)
        at = pl.ds(pl.multiple_of(g * (share * rows), share * rows), share * rows)
        dv = nn(p_s[...], do_s[at]).reshape(blocks, rows, WIDTH)
        dk = (nn(ds_s[...], q_s[at]) * scale).reshape(blocks, rows, WIDTH)
        own_s[g, 0] = dk[REACH]
        own_s[g, 1] = dv[REACH]
        for k in range(1, blocks):
            part_s[g, k, 0] = dk[REACH - k].astype(BF16)
            part_s[g, k, 1] = dv[REACH - k].astype(BF16)
        o_t = nn(v_all.T, p_s[...])
        dq_t = nn(k_all.T, ds_s[...]) * scale
        for h in range(share):
            cols = pl.ds(pl.multiple_of((g * share + h) * WIDTH, WIDTH), WIDTH)
            r = slice(h * rows, (h + 1) * rows)
            o_s[:, cols] = o_t[:, r].T.astype(BF16)
            dq_s[:, cols] = dq_t[:, r].T.astype(BF16)

    def store_heads(g):
        cols = pl.ds(pl.multiple_of(g * (share * WIDTH), share * WIDTH), share * WIDTH)
        return (
            pltpu.make_async_copy(o_s.at[:, cols], attended.at[:, cols], store_sem.at[2 * g]),
            pltpu.make_async_copy(dq_s.at[:, cols], query_grad.at[:, cols], store_sem.at[2 * g + 1]),
        )

    @pl.loop(0, kv_heads)
    def _(g):
        give_up(g, FORWARD - 1).wait_recv()
        give_down(g, FORWARD + 2).wait_recv()
        compute(g)
        stage(g, 0)
        for copy in store_heads(g):
            copy.start()
        for s in range(1, FORWARD):

            @pl.when(g >= s)
            def _():
                stage(g - s, s)

    for late in range(1, FORWARD):
        for s in range(late, FORWARD):
            stage(kv_heads - 1 + late - s, s)
    for g in range(kv_heads):
        last_stage(g)

    finals = (
        pltpu.make_async_copy(fin_s.at[0], key_grad, store_sem.at[2 * kv_heads]),
        pltpu.make_async_copy(fin_s.at[1], value_grad, store_sem.at[2 * kv_heads + 1]),
    )
    for copy in finals:
        copy.start()
    for g in range(kv_heads):
        give_first(g).wait_send()
        for k in range(FORWARD):
            give_up(g, k).wait_send()
        for k in range(FORWARD + 2, REACH + 1):
            give_down(g, k).wait_send()
        for s in range(FORWARD):
            back_down(g, FORWARD - s).wait_send()
            back_up(g, FORWARD + 1 + s).wait_send()
        for copy in store_heads(g):
            copy.wait()
    for copy in finals:
        copy.wait()


def per_device(queries, keys, values, out_grad, doc_lengths):
    rows, columns = queries.shape
    heads, kv_heads = columns // WIDTH, keys.shape[1] // WIDTH
    share = heads // kv_heads
    blocks = REACH + 1
    span = blocks * rows
    dims = (lax.axis_size("dp"), lax.axis_size("seq"), rows, heads, kv_heads)
    hbm = pl.BlockSpec(memory_space=pl.ANY)
    vmem = pltpu.VMEM
    return pl.pallas_call(
        functools.partial(kernel, dims),
        out_shape=tuple(jax.ShapeDtypeStruct(a.shape, BF16) for a in (queries, queries, keys, values)),
        in_specs=[pl.BlockSpec(memory_space=pltpu.SMEM)] + [hbm] * 4,
        out_specs=[hbm] * 4,
        scratch_shapes=[
            vmem((heads * rows, WIDTH), BF16),
            vmem((heads * rows, WIDTH), BF16),
            vmem((kv_heads, blocks, 2, rows, WIDTH), BF16),
            vmem((rows, columns), BF16),
            vmem((rows, columns), BF16),
            vmem((span, rows), F32),
            vmem((2, span, 2 * rows), F32),
            vmem((2, span, 2 * rows), F32),
            vmem((span, share * rows), BF16),
            vmem((span, share * rows), BF16),
            vmem((kv_heads, blocks, 2, rows, WIDTH), BF16),
            vmem((kv_heads, 2, rows, WIDTH), F32),
            vmem((kv_heads, 2, blocks, 2, rows, WIDTH), BF16),
            vmem((2, rows, kv_heads * WIDTH), BF16),
            pltpu.SemaphoreType.DMA((2 * heads + 2 * kv_heads,)),
            pltpu.SemaphoreType.DMA((2 * kv_heads + 2,)),
            pltpu.SemaphoreType.DMA((kv_heads, REACH + 2)),
            pltpu.SemaphoreType.DMA((kv_heads, REACH + 1)),
            pltpu.SemaphoreType.DMA((kv_heads, REACH + 1)),
            pltpu.SemaphoreType.DMA((kv_heads, 2, REACH + 1)),
        ],
        compiler_params=pltpu.CompilerParams(
            collective_id=0, has_side_effects=True, vmem_limit_bytes=56 * 1024 * 1024
        ),
    )(doc_lengths, queries, keys, values, out_grad)


def solution(mesh):
    split = P(("dp", "seq"), None)
    return jax.shard_map(
        per_device,
        mesh=mesh,
        in_specs=(split, split, split, split, P()),
        out_specs=(split, split, split, split),
        check_vma=False,
    )
```

time: 593 us -> 90.3 us (0.15)
  the two profiles are of different devices: /device:TPU:8 before, /device:TPU:31 now
where the time goes in v1:
time: 90.3 us; the launch traced here: 90.1 us
  Pallas kernels  84.5 us (94%)
  local copies, waits for them, and re-layouts  5.01 us (6%)
    pallas_call x1, Pallas kernels, per_device(): pl.pallas_call(functools.partial(kernel, dims), out_shape=tuple((jax.Shap...  84.5 us
    unnamed x10, local copies, waits for them, and re-layouts  5.01 us

profile of v1, /device:TPU:31, one launch (start us, length us, event | category | flops | bytes accessed | tf_op | source)
XLA Modules:
  0.0 90.1 jit_solution(18219725468039751128)
XLA Ops:
  0.6 84.5 %shard_map.84 = (bf16[128,4096]{1,0:T(8,128)(2,1)}, bf16[128,4096]{1,0:T(8,128)(2,1)}, bf16[128,512]{1,0:T(8,128)(2,1)}, bf16[128,512]{1,0:T(8,128)(2,1)}) custom-call(s32[64]{0:T(128)} %lengths.1, bf16[128,4096]{1,0:T(8,128)(2,1)} %queries.1, bf16[128,512]{1,0:T(8,128)(2,1)} %keys.1, bf16[128,512]{1,0:T(8,128)(2,1)} %values.1, bf16[128,4096]{1,0:T(8,128)(2,1)} %out_grad.1), custom_call_target="tpu_custom_call" | custom-call | tf_op jit(solution)/shard_map/pallas_call | solution.py:301
  85.1 0.0 copy-start
  85.1 2.4 %copy.13 = bf16[128,4096]{1,0:T(8,128)(2,1)} copy(bf16[128,4096]{1,0:T(8,128)(2,1)} %get-tuple-element.8) | data formatting | bytes 2097152
  87.5 0.0 copy-done
  87.5 0.0 copy-start.2
  87.5 1.0 %copy.14 = bf16[128,4096]{1,0:T(8,128)(2,1)} copy(bf16[128,4096]{1,0:T(8,128)(2,1)S(1)} %copy-done) | data formatting | bytes 2097152
  88.5 0.1 copy-done.2
  88.5 0.0 copy-start.1
  88.5 0.7 copy.15
  89.2 0.3 copy-done.1
  89.5 0.7 copy.16
Async XLA Ops:
  85.1 2.4 %copy-start = (bf16[128,4096]{1,0:T(8,128)(2,1)S(1)}, bf16[128,4096]{1,0:T(8,128)(2,1)}, u32[]{:S(2)}) copy-start(bf16[128,4096]{1,0:T(8,128)(2,1)} %get-tuple-element.9) | copy-start | bytes 3145732
  87.5 1.0 %copy-start.2 = (bf16[128,512]{1,0:T(8,128)(2,1)S(1)}, bf16[128,512]{1,0:T(8,128)(2,1)}, u32[]{:S(2)}) copy-start(bf16[128,512]{1,0:T(8,128)(2,1)} %get-tuple-element.10) | copy-start | bytes 393220
  88.5 1.0 %copy-start.1 = (bf16[128,512]{1,0:T(8,128)(2,1)S(1)}, bf16[128,512]{1,0:T(8,128)(2,1)}, u32[]{:S(2)}) copy-start(bf16[128,512]{1,0:T(8,128)(2,1)} %get-tuple-element.11) | copy-start | bytes 393220
